TPU v7x, 128 devices: a whole 4x4x4 slice. The times are simulated.
128 devices in a mesh: section: 4 (over z), chan: 32 (over x, y, core).
Axes of the slice: x: 4, y: 4, z: 4, core: 2. Of those that a mesh axis runs over, the one named last changes fastest.
Arguments:
- inputs: bfloat16 [4, 256, 4096], P(None, None, 'chan'), may hold values from -6 to 6
- labels: int32 [4, 256], replicated, may hold values from 0 to 2
- conv_weight: bfloat16 [4, 9, 64, 4096], P('section', None, None, 'chan'), may hold values from -0.25 to 0.25
- point_weight: bfloat16 [4, 4096, 4096], P('section', 'chan'), may hold values from -0.1875 to 0.1875
- head_weight: bfloat16 [4096, 3], P('chan'), may hold values from -0.09375 to 0.09375
Outputs:
- grad_point: float32 [4, 4096, 4096], P('section', 'chan')
- grad_conv: float32 [4, 9, 64, 4096], P('section', None, None, 'chan')
All inputs are finite; a program needn't handle non-finite values.
Results may differ from a plain program's by a relative error of at most 0.035.
Values may be sent and summed in bfloat16 or wider, within the bound.
A program may use at most 128 MiB of HBM per device.

v0:
```python
import jax
import jax.numpy as jnp
from jax import lax
from jax.sharding import PartitionSpec as P

CLASSES = 3
LOSS_SCALE = 2048


def from_behind(value, axis, steps):
    count = lax.axis_size(axis)
    leading, last = (max(0, -steps), min(count, count - steps))
    return lax.ppermute(value, axis, [(source, source + steps) for source in range(leading, last)])


def conv_local(field, kernel, groups):
    half = kernel.shape[0] // 2
    return lax.conv_general_dilated(
        field[None],
        kernel,
        (1,),
        [(half, half)],
        dimension_numbers=("NWC", "WIO", "NWC"),
        feature_group_count=groups,
        preferred_element_type=jnp.float32,
    )[0]


def turn_kernel(kernel):
    taps, width, chans = kernel.shape
    shaped = kernel.reshape(taps, width, chans // width, width)
    shaped = jnp.transpose(shaped, (0, 3, 2, 1))[::-1]
    return shaped.reshape(taps, width, chans)


def kernel_grad(field, grads, width, taps):
    half = taps // 2
    steps, chans = field.shape
    padded = jnp.pad(field, ((half, half), (0, 0)))
    grads3 = grads.reshape(steps, chans // width, width)
    pieces = []
    for k in range(taps):
        shifted = padded[k : k + steps].reshape(steps, chans // width, width)
        pieces.append(
            jnp.einsum("tgi,tgo->igo", shifted, grads3, preferred_element_type=jnp.float32).reshape(
                width, chans
            )
        )
    return jnp.stack(pieces)


def local(inputs, labels, conv_weight, point_weight, head_weight):
    micro, steps, local_chans = inputs.shape
    blocks_here, taps, width, unused_chans = conv_weight.shape
    groups = local_chans // width
    section = lax.axis_index("section")
    n_section = lax.axis_size("section")
    last = n_section - 1
    rounds = micro + n_section - 1
    head32 = head_weight.astype(jnp.float32)
    kernels = [conv_weight[0]]
    turned = [turn_kernel(kernels[0])]
    saved = jnp.zeros((blocks_here, micro, steps, local_chans), jnp.bfloat16)
    top_saved = jnp.zeros((micro, steps, local_chans), jnp.bfloat16)
    received = jnp.zeros((steps, local_chans), jnp.bfloat16)
    for step in range(rounds):
        index = step - section
        valid = (index >= 0) & (index < micro)
        clipped = jnp.clip(index, 0, micro - 1)
        state = jnp.where(
            section == 0, lax.dynamic_index_in_dim(inputs, clipped, 0, keepdims=False), received
        )
        b = 0
        slot = jnp.where(
            valid, lax.dynamic_update_index_in_dim(saved[b], state, clipped, 0), saved[b]
        )
        saved = saved.at[b].set(slot)
        conv_out = conv_local(state, kernels[b], groups)
        act = (conv_out * jax.nn.sigmoid(conv_out)).astype(jnp.bfloat16)
        weight_now = point_weight[b]
        partial_mix = jnp.dot(act, weight_now, preferred_element_type=jnp.float32)
        mixed = lax.psum_scatter(
            partial_mix.astype(jnp.bfloat16), "chan", scatter_dimension=1, tiled=True
        ).astype(jnp.float32)
        state = (state.astype(jnp.float32) + mixed).astype(jnp.bfloat16)
        scores = lax.psum(jnp.dot(state, head_weight, preferred_element_type=jnp.float32), "chan")
        label_row = lax.dynamic_index_in_dim(labels, clipped, 0, keepdims=False)
        onehot = (label_row[:, None] == jnp.arange(CLASSES)[None, :]).astype(jnp.float32)
        top = (jax.nn.sigmoid(scores) - onehot) * (LOSS_SCALE / (micro * steps))
        back_top = jnp.dot(top, head32.T, precision=lax.Precision.HIGHEST).astype(jnp.bfloat16)
        top_saved = jnp.where(
            valid & (section == last),
            lax.dynamic_update_index_in_dim(top_saved, back_top, clipped, 0),
            top_saved,
        )
        if step + 1 < rounds:
            received = from_behind(state, "section", 1)
    grad_point = [jnp.zeros(point_weight.shape[1:], jnp.float32)]
    grad_conv = [jnp.zeros(conv_weight.shape[1:], jnp.float32)]
    received = jnp.zeros((steps, local_chans), jnp.bfloat16)
    for step in range(rounds):
        index = step - (last - section)
        valid = (index >= 0) & (index < micro)
        clipped = jnp.clip(index, 0, micro - 1)
        back = jnp.where(
            section == last,
            lax.dynamic_index_in_dim(top_saved, clipped, 0, keepdims=False),
            received,
        )
        b = 0
        state_b = lax.dynamic_index_in_dim(saved[b], clipped, 0, keepdims=False)
        conv_out = conv_local(state_b, kernels[b], groups)
        sig = jax.nn.sigmoid(conv_out)
        act = jnp.where(valid, (conv_out * sig).astype(jnp.bfloat16), jnp.zeros_like(state_b))
        weight_rows = point_weight[b]

        def fold_grad(carry, piece, start, act=act, weight_rows=weight_rows):
            act_grad, grad_rows_acc = carry
            count = piece.shape[1]
            columns = lax.dynamic_slice_in_dim(weight_rows, start, count, 1)
            act_grad = act_grad + lax.dot_general(
                piece, columns, (((1,), (1,)), ((), ())), preferred_element_type=jnp.float32
            )
            old = lax.dynamic_slice_in_dim(grad_rows_acc, start, count, 1)
            fresh = old + lax.dot_general(
                act, piece, (((0,), (0,)), ((), ())), preferred_element_type=jnp.float32
            )
            return (act_grad, lax.dynamic_update_slice_in_dim(grad_rows_acc, fresh, start, 1))

        start_grad = jnp.zeros((steps, local_chans), jnp.float32)
        act_grad, grad_point[b] = fold_grad(
            (start_grad, grad_point[b]),
            lax.all_gather(back, "chan", axis=1, tiled=True),
            jnp.int32(0),
        )
        conv_grad = jnp.where(
            valid,
            (act_grad * sig * (1.0 + conv_out * (1.0 - sig))).astype(jnp.bfloat16),
            jnp.zeros_like(state_b),
        )
        grad_conv[b] = grad_conv[b] + kernel_grad(state_b, conv_grad, width, taps)
        input_grad = conv_local(conv_grad, turned[b], groups)
        back = (back.astype(jnp.float32) + input_grad).astype(jnp.bfloat16)
        if step + 1 < rounds:
            received = from_behind(back, "section", -1)
    return (jnp.stack(grad_point), jnp.stack(grad_conv))


def solution(mesh):
    placed = (
        P(None, None, "chan"),
        P(),
        P("section", None, None, "chan"),
        P("section", "chan", None),
        P("chan", None),
    )
    return jax.shard_map(
        local,
        mesh=mesh,
        in_specs=placed,
        out_specs=(P("section", "chan", None), P("section", None, None, "chan")),
        check_vma=False,
    )
```

profile of v0, /device:TPU:1, one launch (start us, length us, event | category | flops | bytes accessed | tf_op | source)
XLA Modules:
  0.0 1214.2 jit_solution(8191468728960456842)
XLA Ops:
  14.8 80.3 %reduce-scatter.22.cloned.1.call-done = bf16[128,256]{1,0:T(8,128)(2,1)} async-done(((bf16[4096,256]{1,0:T(8,128)(2,1)}), bf16[128,256]{1,0:T(8,128)(2,1)}) %reduce-scatter.22.cloned.1.call-update) | async-done | bytes 65552
  108.2 79.0 %reduce-scatter.24.cloned.1.call-done = bf16[128,256]{1,0:T(8,128)(2,1)} async-done(((bf16[4096,256]{1,0:T(8,128)(2,1)}), bf16[128,256]{1,0:T(8,128)(2,1)}) %reduce-scatter.24.cloned.1.call-update) | async-done | bytes 65552
  200.3 79.0 %reduce-scatter.26.cloned.1.call-done = bf16[128,256]{1,0:T(8,128)(2,1)} async-done(((bf16[4096,256]{1,0:T(8,128)(2,1)}), bf16[128,256]{1,0:T(8,128)(2,1)}) %reduce-scatter.26.cloned.1.call-update) | async-done | bytes 65552
  280.3 3.7 collective-permute-start.2
  292.5 79.0 %reduce-scatter.28.cloned.1.call-done = bf16[128,256]{1,0:T(8,128)(2,1)} async-done(((bf16[4096,256]{1,0:T(8,128)(2,1)}), bf16[128,256]{1,0:T(8,128)(2,1)}) %reduce-scatter.28.cloned.1.call-update) | async-done | bytes 65552
  384.6 78.9 %reduce-scatter.30.cloned.1.call-done = bf16[128,256]{1,0:T(8,128)(2,1)} async-done(((bf16[4096,256]{1,0:T(8,128)(2,1)}), bf16[128,256]{1,0:T(8,128)(2,1)}) %reduce-scatter.30.cloned.1.call-update) | async-done | bytes 65552
  476.7 78.9 %reduce-scatter.32.cloned.1.call-done = bf16[128,256]{1,0:T(8,128)(2,1)} async-done(((bf16[4096,256]{1,0:T(8,128)(2,1)}), bf16[128,256]{1,0:T(8,128)(2,1)}) %reduce-scatter.32.cloned.1.call-update) | async-done | bytes 65552
  556.6 3.3 collective-permute-start.5
  569.4 78.4 %reduce-scatter.34.cloned.1.call-done = bf16[128,256]{1,0:T(8,128)(2,1)} async-done(((bf16[4096,256]{1,0:T(8,128)(2,1)}), bf16[128,256]{1,0:T(8,128)(2,1)}) %reduce-scatter.34.cloned.1.call-update) | async-done | bytes 65552
  648.9 120.9 %all-reduce.7 = (f32[256,3]{0,1:T(4,128)S(1)}, f32[256,3]{0,1:T(4,128)S(1)}, f32[256,3]{0,1:T(4,128)S(1)}, f32[256,3]{0,1:T(4,128)S(1)}, f32[256,3]{0,1:T(4,128)...) all-reduce(f32[256,3]{0,1:T(4,128)S(1)} %fusion.205, ...), channel_id=1, replica_groups=mesh['section'=4,'chan'=32] {'chan'}, use_global_device_ids=true, to_apply=%region_6.7 | all-reduce | flops 5376 | bytes 43008 | tf_op jit(solution)/shard_map/psum | solution.py:86
  775.2 44.3 %all-gather.21.cloned.1.call-done = bf16[1,256,4096]{2,1,0:T(8,128)(2,1)} async-done(((bf16[1,256,128]{2,1,0:T(8,128)(2,1)}), bf16[1,256,4096]{2,1,0:T(8,128)(2,1)}) %all-gather.21.cloned.1.call-update) | async-done | bytes 2097168 | tf_op jit(solution)/shard_map/all_gather | solution.py:133
  825.6 3.7 collective-permute-done.6
  836.5 38.9 %all-gather.9.cloned.1.call-done = bf16[256,4096]{1,0:T(8,128)(2,1)} async-done(((bf16[256,128]{1,0:T(8,128)(2,1)}), bf16[256,4096]{1,0:T(8,128)(2,1)}) %all-gather.9.cloned.1.call-update) | async-done | bytes 2097168 | tf_op jit(solution)/shard_map/all_gather | solution.py:133
  983.7 3.5 convolution_add_fusion.1
  987.4 9.9 all-gather.13.cloned.1.call-done
  1003.7 3.5 collective-permute-done.9
  1011.1 42.2 %all-gather.15.cloned.1.call-done = bf16[256,4096]{1,0:T(8,128)(2,1)} async-done(((bf16[256,128]{1,0:T(8,128)(2,1)}), bf16[256,4096]{1,0:T(8,128)(2,1)}) %all-gather.15.cloned.1.call-update) | async-done | bytes 2097168 | tf_op jit(solution)/shard_map/all_gather | solution.py:133
  1059.6 3.6 collective-permute-done.10
  1098.9 10.2 all-gather.17.cloned.1.call-done
  1112.5 3.7 fusion.204
  1130.3 3.6 fusion.87
  1161.3 3.5 fusion.85
  1164.8 6.8 all-gather.19.cloned.1.call-done
  1203.4 4.0 fusion.4
  (668 shorter events, 334.3 us)
Async XLA Ops:
  7.2 87.9 %reduce-scatter.22.cloned.1.call-start = ((), (), s32[]{:S(2)}) async-start(), calls=%async_computation.14 | async-start | bytes 2162688
  14.5 172.6 %reduce-scatter.24.cloned.1.call-start = ((), (), s32[]{:S(2)}) async-start(), calls=%async_computation.15 | async-start | bytes 2162688
  96.0 4.5 collective-permute-start
  107.2 172.1 %reduce-scatter.26.cloned.1.call-start = ((), (), s32[]{:S(2)}) async-start(), calls=%async_computation.16 | async-start | bytes 2162688
  188.2 4.5 collective-permute-start.1
  199.4 172.1 %reduce-scatter.28.cloned.1.call-start = ((), (), s32[]{:S(2)}) async-start(), calls=%async_computation.17 | async-start | bytes 2162688
  280.3 4.5 collective-permute-start.2
  291.5 172.0 %reduce-scatter.30.cloned.1.call-start = ((), (), s32[]{:S(2)}) async-start(), calls=%async_computation.18 | async-start | bytes 2162688
  372.4 4.5 collective-permute-start.3
  383.7 172.0 %reduce-scatter.32.cloned.1.call-start = ((), (), s32[]{:S(2)}) async-start(), calls=%async_computation.19 | async-start | bytes 2162688
  475.7 172.1 %reduce-scatter.34.cloned.1.call-start = ((), (), s32[]{:S(2)}) async-start(), calls=%async_computation.20 | async-start | bytes 2162688
  567.9 251.6 %all-gather.21.cloned.1.call-start = ((), (), s32[]{:S(2)}) async-start(), calls=%async_computation.13 | async-start | bytes 2162688 | tf_op jit(solution)/shard_map/all_gather | solution.py:133
  772.9 102.4 %all-gather.9.cloned.1.call-start = ((), (), s32[]{:S(2)}) async-start(), calls=%async_computation.7 | async-start | bytes 2162688 | tf_op jit(solution)/shard_map/all_gather | solution.py:133
  824.3 5.0 collective-permute-start.6
  830.0 110.3 %all-gather.11.cloned.1.call-start = ((), (), s32[]{:S(2)}) async-start(), calls=%async_computation.8 | async-start | bytes 2162688 | tf_op jit(solution)/shard_map/all_gather | solution.py:133
  880.1 5.0 collective-permute-start.7
  885.8 111.5 %all-gather.13.cloned.1.call-start = ((), (), s32[]{:S(2)}) async-start(), calls=%async_computation.9 | async-start | bytes 2162688 | tf_op jit(solution)/shard_map/all_gather | solution.py:133
  945.1 5.0 collective-permute-start.8
  950.7 102.6 %all-gather.15.cloned.1.call-start = ((), (), s32[]{:S(2)}) async-start(), calls=%async_computation.10 | async-start | bytes 2162688 | tf_op jit(solution)/shard_map/all_gather | solution.py:133
  1002.3 5.0 collective-permute-start.9
  1007.9 101.3 %all-gather.17.cloned.1.call-start = ((), (), s32[]{:S(2)}) async-start(), calls=%async_computation.11 | async-start | bytes 2162688 | tf_op jit(solution)/shard_map/all_gather | solution.py:133
  1058.2 5.0 collective-permute-start.10
  1063.8 107.8 %all-gather.19.cloned.1.call-start = ((), (), s32[]{:S(2)}) async-start(), calls=%async_computation.12 | async-start | bytes 2162688 | tf_op jit(solution)/shard_map/all_gather | solution.py:133
  1120.5 5.0 collective-permute-start.11
  (84 other events, 2398.6 us)
Sparse Core Ops, SparseCore 0:
  14.7 80.3 reduce-scatter.21
  107.3 79.7 reduce-scatter.23
  199.5 79.7 reduce-scatter.25
  291.6 79.7 reduce-scatter.27
  383.8 79.7 reduce-scatter.29
  475.9 79.7 reduce-scatter.31
  568.0 79.7 reduce-scatter.33
  773.1 46.3 all-gather.20
  830.1 45.2 all-gather.8
  885.9 45.2 all-gather.10
  950.9 46.3 all-gather.12
  1008.0 45.2 all-gather.14
  1063.9 45.2 all-gather.16
  1126.3 45.2 all-gather.18
where the time goes:
time: 1230 us; the launch traced here: 1210 us
  waiting for transfers between devices  730 us (59%)
  local copies, waits for them, and re-layouts  175 us (14%)
  matrix products  124 us (10%)
  blocking collectives  121 us (10%)
  starting transfers between devices  29 us (2%)
  other arithmetic  18.1 us (1%)
  between operations  17.1 us (1%)
    unnamed x21, waiting for transfers between devices  554 us
    all_gather x7, waiting for transfers between devices, local(): lax.all_gather(back, 'chan', axis=1, tiled=True)  152 us
    psum x1, blocking collectives, local(): lax.psum(jnp.dot(state, head_weight, preferred_element_type=jnp.float32),...  121 us
    unnamed x234, local copies, waits for them, and re-layouts  71.9 us
    another operation x70, local copies, waits for them, and re-layouts, kernel_grad(): return jnp.stack(pieces)  44.8 us
    dot_general x63, matrix products, kernel_grad(): jnp.einsum('tgi,tgo->igo', shifted, grads3, preferred_element_type=jnp.fl...  41.1 us
    conv_general_dilated x20, matrix products, conv_local(): lax.conv_general_dilated(field[None], kernel, (1,), [(half, half)], dimen...  37 us
    slice x63, local copies, waits for them, and re-layouts, kernel_grad(): shifted = padded[k:k + steps].reshape(steps, chans // width, width)  36 us
  transfers between devices with their start and end apart: 26, of which 25 were waited for; matrix products, arithmetic and copies ran while one was open for 15% of the time, Pallas kernels for 0%

commit v1 on v0

--- a/solution.py
+++ b/solution.py
@@ -83,7 +83,10 @@
             partial_mix.astype(jnp.bfloat16), "chan", scatter_dimension=1, tiled=True
         ).astype(jnp.float32)
         state = (state.astype(jnp.float32) + mixed).astype(jnp.bfloat16)
-        scores = lax.psum(jnp.dot(state, head_weight, preferred_element_type=jnp.float32), "chan")
+        scores = jnp.sum(
+            lax.all_gather(jnp.dot(state, head_weight, preferred_element_type=jnp.float32), "chan"),
+            axis=0,
+        )
         label_row = lax.dynamic_index_in_dim(labels, clipped, 0, keepdims=False)
         onehot = (label_row[:, None] == jnp.arange(CLASSES)[None, :]).astype(jnp.float32)
         top = (jax.nn.sigmoid(scores) - onehot) * (LOSS_SCALE / (micro * steps))

time: 1230 us -> 1170 us (0.951)
  waiting for transfers between devices: 730 us -> 622 us
  blocking collectives: 121 us -> 169 us
    all_gather x0 -> x7, blocking collectives: none -> 169 us  [local(): lax.all_gather(jnp.dot(state, head_weight, preferred_element_type=jnp.flo...]
    psum x1 -> x0, blocking collectives: 121 us -> none  [local(): lax.psum(jnp.dot(state, head_weight, preferred_element_type=jnp.float32),...]
    unnamed x21, waiting for transfers between devices: 554 us -> 449 us
    unnamed x234 -> x242, local copies, waits for them, and re-layouts: 71.9 us -> 71.1 us
  transfers between devices with their start and end apart: 26 -> 26, of which waited for: 25 -> 24; matrix products, arithmetic and copies ran while one was open for 15% -> 16% of each run, Pallas kernels for 0% -> 0%
where the time goes in v1:
time: 1170 us; the launch traced here: 1160 us
  waiting for transfers between devices  622 us (53%)
  local copies, waits for them, and re-layouts  175 us (15%)
  blocking collectives  169 us (14%)
  matrix products  124 us (11%)
  starting transfers between devices  29.1 us (2%)
  other arithmetic  17.8 us (2%)
  between operations  17.4 us (1%)
    unnamed x21, waiting for transfers between devices  449 us
    all_gather x7, blocking collectives, local(): lax.all_gather(jnp.dot(state, head_weight, preferred_element_type=jnp.flo...  169 us
    all_gather x7, waiting for transfers between devices, local(): lax.all_gather(back, 'chan', axis=1, tiled=True)  150 us
    unnamed x242, local copies, waits for them, and re-layouts  71.1 us
    another operation x70, local copies, waits for them, and re-layouts, kernel_grad(): return jnp.stack(pieces)  45.1 us
    dot_general x63, matrix products, kernel_grad(): jnp.einsum('tgi,tgo->igo', shifted, grads3, preferred_element_type=jnp.fl...  41.1 us
    conv_general_dilated x20, matrix products, conv_local(): lax.conv_general_dilated(field[None], kernel, (1,), [(half, half)], dimen...  37.1 us
    slice x63, local copies, waits for them, and re-layouts, kernel_grad(): shifted = padded[k:k + steps].reshape(steps, chans // width, width)  36.4 us
  transfers between devices with their start and end apart: 26, of which 24 were waited for; matrix products, arithmetic and copies ran while one was open for 16% of the time, Pallas kernels for 0%

profile of v1, /device:TPU:1, one launch (start us, length us, event | category | flops | bytes accessed | tf_op | source)
XLA Modules:
  0.0 1155.1 jit_solution(9836524677596589428)
XLA Ops:
  14.8 80.3 %reduce-scatter.22.cloned.1.call-done = bf16[128,256]{1,0:T(8,128)(2,1)} async-done(((bf16[4096,256]{1,0:T(8,128)(2,1)}), bf16[128,256]{1,0:T(8,128)(2,1)}) %reduce-scatter.22.cloned.1.call-update) | async-done | bytes 65552
  106.8 79.8 %reduce-scatter.24.cloned.1.call-done = bf16[128,256]{1,0:T(8,128)(2,1)} async-done(((bf16[4096,256]{1,0:T(8,128)(2,1)}), bf16[128,256]{1,0:T(8,128)(2,1)}) %reduce-scatter.24.cloned.1.call-update) | async-done | bytes 65552
  199.7 79.0 %reduce-scatter.26.cloned.1.call-done = bf16[128,256]{1,0:T(8,128)(2,1)} async-done(((bf16[4096,256]{1,0:T(8,128)(2,1)}), bf16[128,256]{1,0:T(8,128)(2,1)}) %reduce-scatter.26.cloned.1.call-update) | async-done | bytes 65552
  279.7 3.7 collective-permute-start.2
  291.9 78.9 %reduce-scatter.28.cloned.1.call-done = bf16[128,256]{1,0:T(8,128)(2,1)} async-done(((bf16[4096,256]{1,0:T(8,128)(2,1)}), bf16[128,256]{1,0:T(8,128)(2,1)}) %reduce-scatter.28.cloned.1.call-update) | async-done | bytes 65552
  384.0 79.0 %reduce-scatter.30.cloned.1.call-done = bf16[128,256]{1,0:T(8,128)(2,1)} async-done(((bf16[4096,256]{1,0:T(8,128)(2,1)}), bf16[128,256]{1,0:T(8,128)(2,1)}) %reduce-scatter.30.cloned.1.call-update) | async-done | bytes 65552
  476.6 26.9 %all-gather = f32[8192,3]{0,1:T(4,128)S(1)} all-gather(f32[256,3]{0,1:T(4,128)S(1)} %fusion.205), channel_id=2, replica_groups=mesh['section'=4,'chan'=32] {'chan'}, dimensions={0}, use_global_device_ids=true | all-gather | bytes 101376 | tf_op jit(solution)/shard_map/all_gather | solution.py:87
  503.7 51.5 %reduce-scatter.32.cloned.1.call-done = bf16[128,256]{1,0:T(8,128)(2,1)} async-done(((bf16[4096,256]{1,0:T(8,128)(2,1)}), bf16[128,256]{1,0:T(8,128)(2,1)}) %reduce-scatter.32.cloned.1.call-update) | async-done | bytes 65552
  568.4 26.9 %all-gather.1 = f32[8192,3]{0,1:T(4,128)S(1)} all-gather(f32[256,3]{0,1:T(4,128)S(1)} %fusion.206), channel_id=3, replica_groups=mesh['section'=4,'chan'=32] {'chan'}, dimensions={0}, use_global_device_ids=true | all-gather | bytes 101376 | tf_op jit(solution)/shard_map/all_gather | solution.py:87
  595.8 22.4 %all-gather.2 = f32[8192,3]{0,1:T(4,128)S(1)} all-gather(f32[256,3]{0,1:T(4,128)S(1)} %fusion.207), channel_id=4, replica_groups=mesh['section'=4,'chan'=32] {'chan'}, dimensions={0}, use_global_device_ids=true | all-gather | bytes 101376 | tf_op jit(solution)/shard_map/all_gather | solution.py:87
  618.7 23.9 %all-gather.3 = f32[8192,3]{0,1:T(4,128)S(1)} all-gather(f32[256,3]{0,1:T(4,128)S(1)} %fusion.208), channel_id=5, replica_groups=mesh['section'=4,'chan'=32] {'chan'}, dimensions={0}, use_global_device_ids=true | all-gather | bytes 101376 | tf_op jit(solution)/shard_map/all_gather | solution.py:87
  643.2 22.4 %all-gather.4 = f32[8192,3]{0,1:T(4,128)S(1)} all-gather(f32[256,3]{0,1:T(4,128)S(1)} %fusion.209), channel_id=6, replica_groups=mesh['section'=4,'chan'=32] {'chan'}, dimensions={0}, use_global_device_ids=true | all-gather | bytes 101376 | tf_op jit(solution)/shard_map/all_gather | solution.py:87
  666.0 23.9 %all-gather.5 = f32[8192,3]{0,1:T(4,128)S(1)} all-gather(f32[256,3]{0,1:T(4,128)S(1)} %fusion.210), channel_id=7, replica_groups=mesh['section'=4,'chan'=32] {'chan'}, dimensions={0}, use_global_device_ids=true | all-gather | bytes 101376 | tf_op jit(solution)/shard_map/all_gather | solution.py:87
  691.5 22.4 %all-gather.6 = f32[8192,3]{0,1:T(4,128)S(1)} all-gather(f32[256,3]{0,1:T(4,128)S(1)} %fusion.76), channel_id=8, replica_groups=mesh['section'=4,'chan'=32] {'chan'}, dimensions={0}, use_global_device_ids=true | all-gather | bytes 101376 | tf_op jit(solution)/shard_map/all_gather | solution.py:87
  717.6 41.9 %all-gather.28.cloned.1.call-done = bf16[1,256,4096]{2,1,0:T(8,128)(2,1)} async-done(((bf16[1,256,128]{2,1,0:T(8,128)(2,1)}), bf16[1,256,4096]{2,1,0:T(8,128)(2,1)}) %all-gather.28.cloned.1.call-update) | async-done | bytes 2097168 | tf_op jit(solution)/shard_map/all_gather | solution.py:136
  765.7 3.7 collective-permute-done.6
  776.4 39.1 %all-gather.16.cloned.1.call-done = bf16[256,4096]{1,0:T(8,128)(2,1)} async-done(((bf16[256,128]{1,0:T(8,128)(2,1)}), bf16[256,4096]{1,0:T(8,128)(2,1)}) %all-gather.16.cloned.1.call-update) | async-done | bytes 2097168 | tf_op jit(solution)/shard_map/all_gather | solution.py:136
  928.1 9.6 all-gather.20.cloned.1.call-done
  951.5 42.2 %all-gather.22.cloned.1.call-done = bf16[256,4096]{1,0:T(8,128)(2,1)} async-done(((bf16[256,128]{1,0:T(8,128)(2,1)}), bf16[256,4096]{1,0:T(8,128)(2,1)}) %all-gather.22.cloned.1.call-update) | async-done | bytes 2097168 | tf_op jit(solution)/shard_map/all_gather | solution.py:136
  1039.6 10.0 all-gather.24.cloned.1.call-done
  1052.9 3.7 fusion.204
  1070.8 3.6 fusion.87
  1105.4 6.7 all-gather.26.cloned.1.call-done
  1144.0 4.0 fusion.4
  (689 shorter events, 352.1 us)
Async XLA Ops:
  7.2 87.9 %reduce-scatter.22.cloned.1.call-start = ((), (), s32[]{:S(2)}) async-start(), calls=%async_computation.14 | async-start | bytes 2162688
  14.5 172.0 %reduce-scatter.24.cloned.1.call-start = ((), (), s32[]{:S(2)}) async-start(), calls=%async_computation.15 | async-start | bytes 2162688
  96.0 4.5 collective-permute-start
  106.6 172.1 %reduce-scatter.26.cloned.1.call-start = ((), (), s32[]{:S(2)}) async-start(), calls=%async_computation.16 | async-start | bytes 2162688
  198.8 172.1 %reduce-scatter.28.cloned.1.call-start = ((), (), s32[]{:S(2)}) async-start(), calls=%async_computation.17 | async-start | bytes 2162688
  279.7 4.5 collective-permute-start.2
  290.9 172.0 %reduce-scatter.30.cloned.1.call-start = ((), (), s32[]{:S(2)}) async-start(), calls=%async_computation.18 | async-start | bytes 2162688
  383.0 172.1 %reduce-scatter.32.cloned.1.call-start = ((), (), s32[]{:S(2)}) async-start(), calls=%async_computation.19 | async-start | bytes 2162688
  464.0 4.5 collective-permute-start.4
  475.2 215.2 %reduce-scatter.34.cloned.1.call-start = ((), (), s32[]{:S(2)}) async-start(), calls=%async_computation.20 | async-start | bytes 2162688
  556.1 4.5 collective-permute-start.5
  567.5 192.1 %all-gather.28.cloned.1.call-start = ((), (), s32[]{:S(2)}) async-start(), calls=%async_computation.13 | async-start | bytes 2162688 | tf_op jit(solution)/shard_map/all_gather | solution.py:136
  715.0 100.5 %all-gather.16.cloned.1.call-start = ((), (), s32[]{:S(2)}) async-start(), calls=%async_computation.7 | async-start | bytes 2162688 | tf_op jit(solution)/shard_map/all_gather | solution.py:136
  764.4 5.0 collective-permute-start.6
  770.0 110.6 %all-gather.18.cloned.1.call-start = ((), (), s32[]{:S(2)}) async-start(), calls=%async_computation.8 | async-start | bytes 2162688 | tf_op jit(solution)/shard_map/all_gather | solution.py:136
  820.2 5.0 collective-permute-start.7
  825.9 111.8 %all-gather.20.cloned.1.call-start = ((), (), s32[]{:S(2)}) async-start(), calls=%async_computation.9 | async-start | bytes 2162688 | tf_op jit(solution)/shard_map/all_gather | solution.py:136
  885.5 5.0 collective-permute-start.8
  891.2 102.6 %all-gather.22.cloned.1.call-start = ((), (), s32[]{:S(2)}) async-start(), calls=%async_computation.10 | async-start | bytes 2162688 | tf_op jit(solution)/shard_map/all_gather | solution.py:136
  942.7 5.0 collective-permute-start.9
  948.4 101.3 %all-gather.24.cloned.1.call-start = ((), (), s32[]{:S(2)}) async-start(), calls=%async_computation.11 | async-start | bytes 2162688 | tf_op jit(solution)/shard_map/all_gather | solution.py:136
  998.6 5.0 collective-permute-start.10
  1004.3 107.8 %all-gather.26.cloned.1.call-start = ((), (), s32[]{:S(2)}) async-start(), calls=%async_computation.12 | async-start | bytes 2162688 | tf_op jit(solution)/shard_map/all_gather | solution.py:136
  1061.0 5.0 collective-permute-start.11
  (88 other events, 2747.0 us)
Sparse Core Ops, SparseCore 0:
  14.7 80.3 reduce-scatter.21
  106.7 79.7 reduce-scatter.23
  198.9 79.7 reduce-scatter.25
  291.0 79.7 reduce-scatter.27
  383.2 79.7 reduce-scatter.29
  475.3 79.7 reduce-scatter.31
  567.6 79.8 reduce-scatter.33
  715.1 44.4 all-gather.27
  770.2 45.2 all-gather.15
  826.1 45.2 all-gather.17
  891.3 46.3 all-gather.19
  948.5 45.2 all-gather.21
  1004.4 45.2 all-gather.23
  1066.8 45.2 all-gather.25
